TPU v7x, 256 devices: a whole 4x4x8 slice. The times are simulated.
256 devices in a mesh: dp: 2 (over z_hi), pipe: 16 (over x, z_lo), tensor: 8 (over y, core).
Axes of the slice: x: 4, y: 4, z: 8 (z_hi: 2, z_lo: 4; z = z_hi * 4 + z_lo), core: 2. Of those that a mesh axis runs over, the one named last changes fastest.
Arguments:
- upstream: bfloat16 [16, 2, 1024, 6144], P('pipe', 'dp', 'tensor')
- inputs: bfloat16 [16, 2, 1024, 6144], P('pipe', 'dp', 'tensor')
- keys: bfloat16 [16, 2, 1024, 6144], P('pipe', 'dp', None, 'tensor')
- values: bfloat16 [16, 2, 1024, 6144], P('pipe', 'dp', None, 'tensor'), may hold values from -6 to 6
- gain: float32 [16, 6144], P('pipe'), may hold values from 0.5 to 1.5
Outputs:
- grad_inputs: bfloat16 [16, 2, 1024, 6144], P('pipe', 'dp', 'tensor')
- grad_keys: bfloat16 [16, 2, 1024, 6144], P('pipe', 'dp', None, 'tensor')
- grad_values: bfloat16 [16, 2, 1024, 6144], P('pipe', 'dp', None, 'tensor')
- grad_gain: float32 [16, 6144], P('pipe', 'tensor')
All inputs are finite; a program needn't handle non-finite values.
Results may differ from a plain program's by a relative error of at most 0.02.
The roundings to bfloat16 on the way count: a program that leaves them out, or rounds other values in their place, can miss the bound.
Values may be sent and summed in bfloat16 or wider, within the bound.
A program may use at most 192 MiB of HBM per device.

v0:
```python
import math

import jax
import jax.numpy as jnp
from jax import lax
from jax.sharding import PartitionSpec as P

HEAD_DIM = 128


EPSILON = 1e-05


def from_behind(x, axis, by):
    devices = lax.axis_size(axis)
    return lax.ppermute(x, axis, [(i, (i + by) % devices) for i in range(devices)])


def attention_back(queries, key_heads, value_heads, grad_out):
    length = queries.shape[1]
    block_rows = min(512, length)
    block_total = length // block_rows
    scaling = 1.0 / math.sqrt(queries.shape[3])
    key_positions = jnp.arange(length)

    def block_step(totals, position):
        acc_keys, acc_values = totals
        offset = position * block_rows
        query_block = lax.dynamic_slice_in_dim(queries, offset, block_rows, 1)
        grad_block = lax.dynamic_slice_in_dim(grad_out, offset, block_rows, 1)
        scores = (
            jnp.einsum(
                "mqhd,mkhd->mhqk", query_block, key_heads, preferred_element_type=jnp.float32
            )
            * scaling
        )
        causal = (offset + jnp.arange(block_rows))[:, None] >= key_positions[None, :]
        scores = jnp.where(causal[None, None], scores, -jnp.inf)
        row_max = jnp.max(scores, axis=-1, keepdims=True)
        log_total = row_max + jnp.log(jnp.sum(jnp.exp(scores - row_max), axis=-1, keepdims=True))
        softmax_weights = jnp.exp(scores - log_total)
        weights_narrow = softmax_weights.astype(jnp.bfloat16)
        grad_weights = jnp.einsum(
            "mqhd,mkhd->mhqk", grad_block, value_heads, preferred_element_type=jnp.float32
        )
        row_delta = jnp.sum(softmax_weights * grad_weights, axis=-1, keepdims=True)
        grad_scores = (softmax_weights * (grad_weights - row_delta) * scaling).astype(jnp.bfloat16)
        acc_values = acc_values + jnp.einsum(
            "mhqk,mqhd->mkhd", weights_narrow, grad_block, preferred_element_type=jnp.float32
        )
        acc_keys = acc_keys + jnp.einsum(
            "mhqk,mqhd->mkhd", grad_scores, query_block, preferred_element_type=jnp.float32
        )
        grad_query = jnp.einsum(
            "mhqk,mkhd->mqhd", grad_scores, key_heads, preferred_element_type=jnp.float32
        ).astype(jnp.bfloat16)
        return ((acc_keys, acc_values), grad_query)

    empty_grads = jnp.zeros(key_heads.shape, jnp.float32)
    (grad_keys, grad_values), grad_blocks = lax.scan(
        block_step, (empty_grads, empty_grads), jnp.arange(block_total)
    )
    grad_queries = jnp.moveaxis(grad_blocks, 0, 1).reshape(queries.shape)
    return (grad_queries, grad_keys, grad_values)


def body(upstream, inputs, keys, values, gain):
    tensor_size = lax.axis_size("tensor")
    tensor_rank = lax.axis_index("tensor")
    batches = inputs.shape[1]
    tokens_local = inputs.shape[2]
    columns = inputs.shape[3] // tensor_size
    length = keys.shape[2]
    inputs_wide = inputs.astype(jnp.float32)
    root_mean = jnp.sqrt(jnp.mean(inputs_wide * inputs_wide, axis=-1, keepdims=True) + EPSILON)
    normed = inputs_wide / root_mean
    normed_b = normed.astype(jnp.bfloat16)
    normed_heads = lax.all_to_all(normed_b, "tensor", split_axis=3, concat_axis=2, tiled=True)
    full_rows = lax.all_gather(upstream, "tensor", axis=2, tiled=True)
    arrived = from_behind(full_rows, "pipe", -1)
    incoming = lax.dynamic_slice_in_dim(arrived, tensor_rank * tokens_local, tokens_local, 2)
    grad_out = lax.dynamic_slice_in_dim(arrived, tensor_rank * columns, columns, 3)
    gain_columns = lax.dynamic_slice_in_dim(gain, tensor_rank * columns, columns, 1)
    queries = (normed_heads.astype(jnp.float32) * gain_columns[:, None, None, :]).astype(
        jnp.bfloat16
    )
    head_shape = (batches, length, columns // HEAD_DIM, HEAD_DIM)
    grad_queries, grad_keys, grad_values = attention_back(
        queries[0].reshape(head_shape),
        keys[0].reshape(head_shape),
        values[0].reshape(head_shape),
        grad_out[0].reshape(head_shape),
    )
    grad_flat = grad_queries.reshape(1, batches, length, columns)
    partial_gain = jnp.sum(
        grad_flat.astype(jnp.float32) * normed_heads.astype(jnp.float32), axis=(1, 2)
    )
    grad_gain = lax.psum(partial_gain, "dp")
    grad_rows = lax.all_to_all(grad_flat, "tensor", split_axis=2, concat_axis=3, tiled=True)
    scaled = grad_rows.astype(jnp.float32) * gain[:, None, None, :]
    grad_inputs = (
        incoming.astype(jnp.float32)
        + (scaled - normed * jnp.mean(scaled * normed, axis=-1, keepdims=True)) / root_mean
    )
    return (
        grad_inputs.astype(jnp.bfloat16),
        grad_keys.reshape(keys.shape).astype(jnp.bfloat16),
        grad_values.reshape(values.shape).astype(jnp.bfloat16),
        grad_gain,
    )


def solution(mesh):
    in_specs = (
        P("pipe", "dp", "tensor", None),
        P("pipe", "dp", "tensor", None),
        P("pipe", "dp", None, "tensor"),
        P("pipe", "dp", None, "tensor"),
        P("pipe", None),
    )
    out_specs = (
        P("pipe", "dp", "tensor", None),
        P("pipe", "dp", None, "tensor"),
        P("pipe", "dp", None, "tensor"),
        P("pipe", "tensor"),
    )
    return jax.shard_map(body, mesh=mesh, in_specs=in_specs, out_specs=out_specs, check_vma=False)
```

profile of v0, /device:TPU:1, one launch (start us, length us, event | category | flops | bytes accessed | tf_op | source)
XLA Modules:
  0.0 637.2 jit_solution(1823012857583633548)
XLA Ops:
  9.9 79.4 %all-gather.2.cloned.1.call-done = bf16[1,1,1024,6144]{2,3,1,0:T(8,128)(2,1)} async-done(((bf16[1,1,128,6144]{2,3,1,0:T(8,128)(2,1)}), bf16[1,1,1024,6144]{2,3,1,0:T(8,128)(2,1)}) %all-gather.2.cloned.1.call-update) | async-done | bytes 12582928 | tf_op jit(solution)/shard_map/all_gather | solution.py:79
  89.3 5.4 collective-permute-start
  96.8 25.2 %copy.80 = bf16[1,1,128,6144]{2,1,0,3:T(2,128)(2,1)} copy(bf16[1,1,128,6144]{2,3,1,0:T(8,128)(2,1)S(1)} %fusion.85) | data formatting | bytes 3145728 | tf_op jit(solution)/shard_map/convert_element_type | solution.py:77
  122.5 34.3 %reduce.11 = bf16[6144,128]{1,0:T(8,128)(2,1)S(1)} reduce(bf16[6144,1,1,128]{3,2,1,0:T(2,128)(2,1)} %bitcast.111, bf16[]{:T(256)} %broadcast.156), dimensions={1,2}, to_apply=%bitcast.87.reduce_sub_computation | reduce | bytes 3145730
  158.7 5.3 all-to-all-start
  169.8 15.0 %all-to-all-done = bf16[8,2,49152]{2,1,0:T(2,128)(2,1)} async-done(((bf16[8,2,49152]{2,1,0:T(2,128)(2,1)}), bf16[8,2,49152]{2,1,0:T(2,128)(2,1)}, u32[]{:S(2)}, u32[]{:S(2)}) %all-to-all-start) | async-done | bytes 1572896 | tf_op jit(solution)/shard_map/all_to_all | solution.py:78
  184.8 6.4 reshape.278
  195.3 4.1 multiply_convert_fusion.1
  199.4 8.2 %copy.58 = bf16[1,1024,6,128]{3,1,2,0:T(8,128)(2,1)} copy(bf16[1,1024,6,128]{1,0,3,2:T(2,128)(2,1)} %multiply_convert_fusion.1) | data formatting | bytes 3145728
  207.6 156.9 %collective-permute-done = bf16[1,1,1024,6144]{2,3,1,0:T(8,128)(2,1)} collective-permute-done((bf16[1,1,1024,6144]{2,3,1,0:T(8,128)(2,1)}, bf16[1,1,1024,6144]{2,3,1,0:T(8,128)(2,1)}, u32[]{:S(2)}, u32[]{:S(2)}) %collective-permute-start) | collective-permute-done | bytes 12582944 | tf_op jit(solution)/shard_map/ppermute | solution.py:16
  367.2 176.9 %while.15 = (s32[]{:T(128)}, f32[1,1024,6,128]{1,3,2,0:T(8,128)}, f32[1,1024,6,128]{1,3,2,0:T(8,128)}, bf16[2,1,512,6,128]{4,2,3,1,0:T(8,128)(2,1)}, s32[2]{0:T(...) while((s32[]{:T(128)}, f32[1,1024,6,128]{1,3,2,0:T(8,128)}, ...), condition=%wide.region_5.6_spmd.clone, body=%wide.region_1.5_spmd.clone.sunk | while | flops 4134409728 | bytes 233201936 | solution.py:60
  369.0 8.2 %fusion.105 = f32[6,512,1024]{2,1,0:T(8,128)} fusion(bf16[1,1024,6,128]{3,1,2,0:T(8,128)(2,1)} %get-tuple-element.245, bf16[1,1024,6,128]{1,3,2,0:T(8,128)(2,1)} %get-tuple-element.244, s32[]{:T(128)S(6)} %select_n.79), kind=kOutput, calls=%fused_computation.28.clone.1 | convolution fusion | flops 805306368 | bytes 14942212 | tf_op jit(solution)/shard_map/while/body/eval_jaxpr/mqhd,mkhd->mhqk/dot_general | solution.py:43
  379.5 3.7 exponential_reduce_fusion.2
  383.9 25.5 %fusion.107 = bf16[2,1,512,6,128]{4,2,3,1,0:T(8,128)(2,1)} fusion(bf16[2,1,512,6,128]{4,2,3,1,0:T(8,128)(2,1)} %get-tuple-element.227, s32[]{:T(128)S(6)} %copy.86, bf16[1,1024,6,128]{3,1,2,0:T(8,128)(2,1)S(1)} %get-tuple-element.243, f32[6,512,1024]{2,1,0:T(8,128)} %fusion.105, f32[6,512,1024]{2,1,0:T(8,128)} %copy-done, ...), kind=kOutput, calls=%fused_computation.35.clone.1 | convolution fusion | flops 840306688 | bytes 53772292 | tf_op jit(solution)/shard_map/while/body/eval_jaxpr/mhqk,mkhd->mqhd/dot_general | solution.py:54
  409.5 35.1 %bitcast_add_fusion.4 = f32[1,1024,6,128]{1,3,2,0:T(8,128)} fusion(f32[1,1024,6,128]{1,3,2,0:T(8,128)} %get-tuple-element.225, f32[6,512,1024]{2,1,0:T(8,128)} %fusion.105, f32[6,512,1024]{2,1,0:T(8,128)} %copy-done, f32[6,512]{1,0:T(8,128)S(1)} %log_add_fusion.2, pred[512,1024]{1,0:T(8,128)(4,1)S(1)} %iota_compare_fusion.2, pred[]{:T(512)S(6)} %compare.3, ...), kind=kOutput, calls=%fused_computation.26.clone.1 | convolution fusion | flops 841486336 | bytes 58490884 | tf_op jit(solution)/shard_map/while/body/eval_jaxpr/mhqk,mqhd->mkhd/dot_general | solution.py:51
  444.6 10.2 %bitcast_add_fusion.5 = f32[1,1024,6,128]{1,3,2,0:T(8,128)} fusion(f32[1,1024,6,128]{1,3,2,0:T(8,128)} %get-tuple-element.226, f32[6,512,1024]{2,1,0:T(8,128)} %copy-done, f32[6,512]{1,0:T(8,128)S(1)} %log_add_fusion.2, pred[512,1024]{1,0:T(8,128)(4,1)S(1)} %iota_compare_fusion.2, pred[]{:T(512)S(6)} %compare.3, ...), kind=kOutput, calls=%fused_computation.25.clone.1 | convolution fusion | flops 819462144 | bytes 20197380 | tf_op jit(solution)/shard_map/while/body/eval_jaxpr/mhqk,mqhd->mkhd/dot_general | solution.py:48
  456.4 8.2 %fusion.105 = f32[6,512,1024]{2,1,0:T(8,128)} fusion(bf16[1,1024,6,128]{3,1,2,0:T(8,128)(2,1)} %get-tuple-element.245, bf16[1,1024,6,128]{1,3,2,0:T(8,128)(2,1)} %get-tuple-element.244, s32[]{:T(128)S(6)} %select_n.79), kind=kOutput, calls=%fused_computation.28.clone.1 | convolution fusion | flops 805306368 | bytes 14942212 | tf_op jit(solution)/shard_map/while/body/eval_jaxpr/mqhd,mkhd->mhqk/dot_general | solution.py:43
  466.9 3.7 exponential_reduce_fusion.2
  471.4 25.5 %fusion.107 = bf16[2,1,512,6,128]{4,2,3,1,0:T(8,128)(2,1)} fusion(bf16[2,1,512,6,128]{4,2,3,1,0:T(8,128)(2,1)} %get-tuple-element.227, s32[]{:T(128)S(6)} %copy.86, bf16[1,1024,6,128]{3,1,2,0:T(8,128)(2,1)S(1)} %get-tuple-element.243, f32[6,512,1024]{2,1,0:T(8,128)} %fusion.105, f32[6,512,1024]{2,1,0:T(8,128)} %copy-done, ...), kind=kOutput, calls=%fused_computation.35.clone.1 | convolution fusion | flops 840306688 | bytes 53772292 | tf_op jit(solution)/shard_map/while/body/eval_jaxpr/mhqk,mkhd->mqhd/dot_general | solution.py:54
  496.9 35.6 %bitcast_add_fusion.4 = f32[1,1024,6,128]{1,3,2,0:T(8,128)} fusion(f32[1,1024,6,128]{1,3,2,0:T(8,128)} %get-tuple-element.225, f32[6,512,1024]{2,1,0:T(8,128)} %fusion.105, f32[6,512,1024]{2,1,0:T(8,128)} %copy-done, f32[6,512]{1,0:T(8,128)S(1)} %log_add_fusion.2, pred[512,1024]{1,0:T(8,128)(4,1)S(1)} %iota_compare_fusion.2, pred[]{:T(512)S(6)} %compare.3, ...), kind=kOutput, calls=%fused_computation.26.clone.1 | convolution fusion | flops 841486336 | bytes 58490884 | tf_op jit(solution)/shard_map/while/body/eval_jaxpr/mhqk,mqhd->mkhd/dot_general | solution.py:51
  532.5 11.2 %bitcast_add_fusion.5 = f32[1,1024,6,128]{1,3,2,0:T(8,128)} fusion(f32[1,1024,6,128]{1,3,2,0:T(8,128)} %get-tuple-element.226, f32[6,512,1024]{2,1,0:T(8,128)} %copy-done, f32[6,512]{1,0:T(8,128)S(1)} %log_add_fusion.2, pred[512,1024]{1,0:T(8,128)(4,1)S(1)} %iota_compare_fusion.2, pred[]{:T(512)S(6)} %compare.3, ...), kind=kOutput, calls=%fused_computation.25.clone.1 | convolution fusion | flops 819462144 | bytes 20197380 | tf_op jit(solution)/shard_map/while/body/eval_jaxpr/mhqk,mqhd->mkhd/dot_general | solution.py:48
  544.1 3.9 copy.73
  548.0 8.6 %reshape.275 = bf16[1,1,1024,768]{3,1,0,2:T(2,128)(2,1)S(1)} reshape(bf16[2,1,512,6,128]{4,3,2,0,1:T(8,128)(2,1)} %copy.73) | data formatting | bytes 3145728 | tf_op jit(solution)/shard_map/reshape;reshape;transpose | solution.py:94
  556.5 11.4 %reduce.12 = bf16[1024,768]{1,0:T(8,128)(2,1)} reduce(bf16[1024,1,1,768]{3,2,1,0:T(2,128)(2,1)S(1)} %bitcast.112, bf16[]{:T(256)} %broadcast.156), dimensions={1,2}, to_apply=%bitcast.79.reduce_sub_computation | reduce | bytes 3145730
  568.0 3.9 reshape.279
  571.8 5.2 all-to-all-start.1
  580.5 3.5 reshape.267
  584.0 4.9 copy.62
  600.7 3.9 multiply_reduce_fusion.1
  604.6 8.3 %psum.7 = f32[1,768]{1,0:T(1,128)} all-reduce(f32[1,768]{1,0:T(1,128)S(1)} %bitcast.126), channel_id=1, replica_groups=mesh['dp'=2,'pipe'=16,'tensor'=8] {'dp'}, use_global_device_ids=true, to_apply=%region_8.9 | all-reduce | flops 768 | bytes 6144 | tf_op jit(solution)/shard_map/psum | solution.py:98
  612.8 4.7 reshape.280
  619.8 3.7 copy.65
  (73 shorter events, 52.0 us)
Async XLA Ops:
  7.2 87.5 %copy-start.7 = (bf16[1,1,128,6144]{3,2,1,0:T(8,128)(2,1)S(1)}, bf16[1,1,128,6144]{3,2,1,0:T(8,128)(2,1)}, u32[]{:S(2)}) copy-start(bf16[1,1,128,6144]{3,2,1,0:T(8,128)(2,1)} %param.8) | copy-start | bytes 4718596
  7.2 82.1 %all-gather.2.cloned.1.call-start = ((), (), s32[]{:S(2)}) async-start(), calls=%async_computation.2 | async-start | bytes 14155776 | tf_op jit(solution)/shard_map/all_gather | solution.py:79
  89.3 275.2 %collective-permute-start = (bf16[1,1,1024,6144]{2,3,1,0:T(8,128)(2,1)}, bf16[1,1,1024,6144]{2,3,1,0:T(8,128)(2,1)}, u32[]{:S(2)}, u32[]{:S(2)}) collective-permute-start(bf16[1,1,1024,6144]{2,3,1,0:T(8,128)(2,1)} %all-gather.2.cloned.1.call-done), channel_id=1, source_target_pairs={{0,120},{8,0},{16,8},{24,16},{32,24},{40,32},{48,40},{56,48},{64,5... | collective-permute-start | bytes 37748744 | tf_op jit(solution)/shard_map/ppermute | solution.py:16
  95.6 26.3 %copy-start.1 = (bf16[1,1,128,6144]{2,3,1,0:T(8,128)(2,1)}, bf16[1,1,128,6144]{2,3,1,0:T(8,128)(2,1)S(1)}, u32[]{:S(2)}) copy-start(bf16[1,1,128,6144]{2,3,1,0:T(8,128)(2,1)S(1)} %copy.52) | copy-start | bytes 4718596
  96.5 25.5 %copy-start.10 = (f32[128]{0:T(128)}, f32[128]{0:T(128)S(1)}, u32[]{:S(2)}) copy-start(f32[128]{0:T(128)S(1)} %add_sqrt_fusion) | copy-start | bytes 1540
  158.7 5.4 copy-start.8
  158.7 26.1 %all-to-all-start = ((bf16[8,2,49152]{2,1,0:T(2,128)(2,1)}), bf16[8,2,49152]{2,1,0:T(2,128)(2,1)}, u32[]{:S(2)}, u32[]{:S(2)}) async-start(bf16[8,2,49152]{2,1,0:T(2,128)(2,1)} %reshape.277), calls=%async_computation | async-start | bytes 3145728 | tf_op jit(solution)/shard_map/all_to_all | solution.py:78
  193.5 1.8 copy-start.3
  369.0 8.2 %copy-start.6 = (bf16[1,1024,6,128]{3,1,2,0:T(8,128)(2,1)S(1)}, bf16[1,1024,6,128]{3,1,2,0:T(8,128)(2,1)}, u32[]{:S(2)}) copy-start(bf16[1,1024,6,128]{3,1,2,0:T(8,128)(2,1)} %get-tuple-element.242) | copy-start | bytes 4718596 | tf_op jit(solution)/shard_map/while
  379.5 4.5 copy-start
  456.4 8.2 %copy-start.6 = (bf16[1,1024,6,128]{3,1,2,0:T(8,128)(2,1)S(1)}, bf16[1,1024,6,128]{3,1,2,0:T(8,128)(2,1)}, u32[]{:S(2)}) copy-start(bf16[1,1024,6,128]{3,1,2,0:T(8,128)(2,1)} %get-tuple-element.242) | copy-start | bytes 4718596 | tf_op jit(solution)/shard_map/while
  466.9 4.5 copy-start
  568.0 9.1 %copy-start.4 = (f32[1,1,8,128,768]{3,4,2,1,0:T(8,128)S(1)}, f32[1,1,8,128,768]{3,4,2,1,0:T(8,128)}, u32[]{:S(2)}) copy-start(f32[1,1,8,128,768]{3,4,2,1,0:T(8,128)} %copy-done.3) | copy-start | bytes 9437188
  571.8 41.0 %all-to-all-start.1 = ((bf16[8,2,49152]{2,1,0:T(2,128)(2,1)}), bf16[8,2,49152]{2,1,0:T(2,128)(2,1)}, u32[]{:S(2)}, u32[]{:S(2)}) async-start(bf16[8,2,49152]{2,1,0:T(2,128)(2,1)} %reshape.279), calls=%async_computation.1 | async-start | bytes 3145728 | tf_op jit(solution)/shard_map/all_to_all | solution.py:99
  619.7 3.7 copy-start.2
  619.7 3.7 copy-start.9
  619.8 3.7 copy-start.11
  623.4 2.8 copy-start.5
Sparse Core Ops, SparseCore 0:
  10.4 78.8 all-gather.1
where the time goes:
time: 647 us; the launch traced here: 637 us
  waiting for transfers between devices  251 us (39%)
  matrix products  164 us (25%)
  local copies, waits for them, and re-layouts  105 us (16%)
  other arithmetic  76.6 us (12%)
  starting transfers between devices  16 us (2%)
  between operations  14.5 us (2%)
  blocking collectives  8.27 us (1%)
    ppermute x1, waiting for transfers between devices, from_behind(): lax.ppermute(x, axis, [(i, (i + by) % devices) for i in range(devices)])  157 us
    all_gather x1, waiting for transfers between devices, body(): full_rows = lax.all_gather(upstream, 'tensor', axis=2, tiled=True)  79.4 us
    dot_general x2, matrix products, block_step(): jnp.einsum('mhqk,mqhd->mkhd', grad_scores, query_block, preferred_element...  70.7 us
    dot_general x2, matrix products, block_step(): jnp.einsum('mhqk,mkhd->mqhd', grad_scores, key_heads, preferred_element_t...  51 us
    unnamed x4, other arithmetic  45.8 us
    unnamed x36, local copies, waits for them, and re-layouts  41 us
    convert_element_type x1, local copies, waits for them, and re-layouts, body(): normed_b = normed.astype(jnp.bfloat16)  25.2 us
    dot_general x2, matrix products, block_step(): jnp.einsum('mhqk,mqhd->mkhd', weights_narrow, grad_block, preferred_eleme...  21.4 us
  transfers between devices with their start and end apart: 4, of which 3 were waited for; matrix products, arithmetic and copies ran while one was open for 19% of the time, Pallas kernels for 0%

commit v1 on v0

v1 whole, which is shorter than its diff:
```python
import functools
import math

import jax
import jax.numpy as jnp
from jax import lax
from jax.experimental import pallas as pl
from jax.experimental.pallas import tpu as pltpu
from jax.sharding import PartitionSpec as P

MESH = pl.DeviceIdType.MESH
HEAD_DIM = 128
EPSILON = 1e-05
ROWS = 256
F32 = jnp.float32
BF16 = jnp.bfloat16

NT = (((1,), (1,)), ((), ()))
NN = (((1,), (0,)), ((), ()))


def dot(a, b, dims):
    return lax.dot_general(a, b, dims, preferred_element_type=F32)


def fold(x, op):
    return op(x.reshape(x.shape[0] // 8, 8, x.shape[1]), axis=0)


def kernel(
    n_pipe, n_t, heads,
    up_hbm, x_hbm, k_hbm, v_hbm, gain_hbm,
    gi_hbm, dk_hbm, dv_hbm, gg_ref,
    x_s, gain_s, inv_s, nb, qn, up, go, dqs, dqr, k_s, v_s, q_s, kt_s,
    s_s, d_s, dk_acc, dv_acc, dk_b, dv_b, acc_s, out_b, pg, pgr,
    x_sem, gain_sem, k_sem, v_sem, nb_send, qn_recv, up_send, up_recv,
    go_send, go_recv, dq_send, dq_recv, pg_send, pg_recv, dk_sem, dv_sem, out_sem,
):
    d = lax.axis_index("dp")
    p = lax.axis_index("pipe")
    t = lax.axis_index("tensor")
    before = lax.rem(p + n_pipe - 1, n_pipe)
    after = lax.rem(p + 1, n_pipe)
    tokens = x_s.shape[0]
    length = n_t * tokens
    width = heads * HEAD_DIM
    features = n_t * width
    mine = pl.ds(pl.multiple_of(t * tokens, tokens), tokens)

    def peer(k):
        return lax.rem(t + k, n_t)

    barrier = pltpu.get_barrier_semaphore()

    def greet(k, carry):
        pl.semaphore_signal(barrier, inc=1, device_id=(d, p, peer(k)), device_id_type=MESH)
        return carry

    lax.fori_loop(1, n_t, greet, 0)
    pl.semaphore_signal(barrier, inc=1, device_id=(d, after, t), device_id_type=MESH)
    pl.semaphore_signal(barrier, inc=1, device_id=(1 - d, p, t), device_id_type=MESH)

    load_x = pltpu.make_async_copy(x_hbm, x_s, x_sem)
    load_x.start()
    load_gain = pltpu.make_async_copy(gain_hbm, gain_s, gain_sem)
    load_gain.start()

    def head_columns(h):
        return pl.ds(pl.multiple_of(h * HEAD_DIM, HEAD_DIM), HEAD_DIM)

    def load_k(h):
        return pltpu.make_async_copy(k_hbm.at[:, head_columns(h)], k_s.at[h], k_sem.at[h])

    def load_v(h):
        return pltpu.make_async_copy(v_hbm.at[:, head_columns(h)], v_s.at[h], v_sem.at[h])

    def start_loads(h, carry):
        load_k(h).start()
        load_v(h).start()
        return carry

    lax.fori_loop(0, heads, start_loads, 0)
    load_x.wait()

    def norm_rows(r, carry):
        rows = pl.ds(pl.multiple_of(r * 16, 16), 16)
        total = jnp.zeros((16, HEAD_DIM), F32)
        for c in range(n_t * heads):
            x = x_s[rows, c * HEAD_DIM : (c + 1) * HEAD_DIM].astype(F32)
            total = total + x * x
        mean = jnp.sum(total, axis=1, keepdims=True) * (1.0 / features)
        inv = jnp.broadcast_to(1.0 / jnp.sqrt(mean + EPSILON), (16, HEAD_DIM))
        inv_s[rows, :] = inv
        for c in range(n_t * heads):
            x = x_s[rows, c * HEAD_DIM : (c + 1) * HEAD_DIM].astype(F32)
            nb[c % heads, c // heads, rows, :] = (x * inv).astype(BF16)
        return carry

    lax.fori_loop(0, tokens // 16, norm_rows, 0)
    pg[...] = jnp.zeros_like(pg)

    pl.semaphore_wait(barrier, n_t + 1)

    def send_round(h, carry):
        def send_normed(k, carry):
            to = peer(k)
            pltpu.make_async_remote_copy(
                src_ref=nb.at[h, to], dst_ref=qn.at[h, mine, :],
                send_sem=nb_send.at[h], recv_sem=qn_recv.at[h],
                device_id=(d, p, to), device_id_type=MESH,
            ).start()
            return carry

        lax.fori_loop(1, n_t, send_normed, 0)
        pltpu.make_async_copy(nb.at[h, t], qn.at[h, mine, :], qn_recv.at[h]).start()

        def send_rows(j, carry):
            columns = pl.ds(pl.multiple_of((j * heads + h) * HEAD_DIM, HEAD_DIM), HEAD_DIM)
            pltpu.make_async_remote_copy(
                src_ref=up_hbm.at[:, columns], dst_ref=up.at[h, j],
                send_sem=up_send.at[h], recv_sem=up_recv.at[h],
                device_id=(d, before, t), device_id_type=MESH,
            ).start()
            return carry

        lax.fori_loop(0, n_t, send_rows, 0)
        return carry

    lax.fori_loop(0, heads, send_round, 0)
    load_gain.wait()

    def relay(h):
        pltpu.make_async_copy(up.at[h], up.at[h], up_recv.at[h]).wait()

        def send_grad(k, carry):
            to = peer(k)
            pltpu.make_async_remote_copy(
                src_ref=up.at[h, to], dst_ref=go.at[h, mine, :],
                send_sem=go_send.at[h], recv_sem=go_recv.at[h],
                device_id=(d, p, to), device_id_type=MESH,
            ).start()
            return carry

        lax.fori_loop(1, n_t, send_grad, 0)
        pltpu.make_async_copy(up.at[h, t], go.at[h, mine, :], go_recv.at[h]).start()

    to_base2 = math.log2(math.e) / math.sqrt(HEAD_DIM)
    scaling = 1.0 / math.sqrt(HEAD_DIM)
    blocks = length // ROWS
    below = lax.broadcasted_iota(jnp.int32, (ROWS, ROWS), 0) <= lax.broadcasted_iota(
        jnp.int32, (ROWS, ROWS), 1
    )

    def row_block(h, i):
        rows = pl.ds(i * ROWS, ROWS)
        q_i = q_s[rows, :]
        g_i = go[h, rows, :]
        top = None
        for c in range(i + 1):
            keys = pl.ds(c * ROWS, ROWS)
            s = dot(k_s[h, keys, :], q_i, NT)
            if c == i:
                s = jnp.where(below, s, -jnp.inf)
            s_s[keys, :] = s
            m = fold(s, jnp.max)
            top = m if top is None else jnp.maximum(top, m)
        top = jnp.max(top, axis=0, keepdims=True)
        total = jnp.zeros((8, ROWS), F32)
        weighted = jnp.zeros((8, ROWS), F32)
        for c in range(i + 1):
            keys = pl.ds(c * ROWS, ROWS)
            e = jnp.exp2((s_s[keys, :] - top) * to_base2)
            dp = dot(v_s[h, keys, :], g_i, NT)
            s_s[keys, :] = e
            d_s[keys, :] = dp
            total = total + fold(e, jnp.sum)
            weighted = weighted + fold(e * dp, jnp.sum)
        norm = 1.0 / jnp.sum(total, axis=0, keepdims=True)
        delta = jnp.sum(weighted, axis=0, keepdims=True) * norm
        norm_scaled = norm * scaling
        dq_t = jnp.zeros((HEAD_DIM, ROWS), F32)
        for c in range(i + 1):
            keys = pl.ds(c * ROWS, ROWS)
            e = s_s[keys, :]
            weights = (e * norm).astype(BF16)
            grad_s = ((e * norm_scaled) * (d_s[keys, :] - delta)).astype(BF16)
            dv = dot(weights, g_i, NN)
            dk = dot(grad_s, q_i, NN)
            if c == i:
                dv_acc[keys, :] = dv
                dk_acc[keys, :] = dk
            else:
                dv_acc[keys, :] += dv
                dk_acc[keys, :] += dk
            dq_t = dq_t + dot(kt_s[:, keys], grad_s, NN)
        dq = dq_t.T.astype(BF16)
        dqs[h, rows, :] = dq
        part = fold(dq.astype(F32) * qn[h, rows, :].astype(F32), jnp.sum)
        pg[pl.ds(h, 1), :] += jnp.sum(part, axis=0, keepdims=True)
        for b in range(ROWS // tokens):
            to = i * (ROWS // tokens) + b
            block = dqs.at[h, pl.ds(to * tokens, tokens), :]

            @pl.when(to != t)
            def _():
                pltpu.make_async_remote_copy(
                    src_ref=block, dst_ref=dqr.at[h, t],
                    send_sem=dq_send.at[h], recv_sem=dq_recv.at[h],
                    device_id=(d, p, to), device_id_type=MESH,
                ).start()

            @pl.when(to == t)
            def _():
                pltpu.make_async_copy(block, dqr.at[h, t], dq_recv.at[h]).start()

    def store_dk(h):
        return pltpu.make_async_copy(dk_b.at[h], dk_hbm.at[:, head_columns(h)], dk_sem.at[h])

    def store_dv(h):
        return pltpu.make_async_copy(dv_b.at[h], dv_hbm.at[:, head_columns(h)], dv_sem.at[h])

    def head(h, carry):
        @pl.when(h + 1 < heads)
        def _():
            relay(h + 1)

        load_k(h).wait()
        load_v(h).wait()
        kt_s[...] = k_s[h].T
        pltpu.make_async_copy(qn.at[h], qn.at[h], qn_recv.at[h]).wait()
        gain_row = gain_s[pl.ds(t * heads + h, 1), :]
        q_s[...] = (qn[h].astype(F32) * gain_row).astype(BF16)
        pltpu.make_async_copy(go.at[h], go.at[h], go_recv.at[h]).wait()
        for i in range(blocks):
            row_block(h, i)
        dk_b[h] = dk_acc[...].astype(BF16)
        dv_b[h] = dv_acc[...].astype(BF16)
        store_dk(h).start()
        store_dv(h).start()
        return carry

    relay(0)
    lax.fori_loop(0, heads, head, 0)

    share = pltpu.make_async_remote_copy(
        src_ref=pg, dst_ref=pgr, send_sem=pg_send, recv_sem=pg_recv,
        device_id=(1 - d, p, t), device_id_type=MESH,
    )
    share.start()

    acc_s[...] = jnp.zeros_like(acc_s)

    def arrived(h, carry):
        pltpu.make_async_copy(dqr.at[h], dqr.at[h], dq_recv.at[h]).wait()
        acc = acc_s[...]
        for j in range(n_t):
            columns = pl.ds(pl.multiple_of((j * heads + h) * HEAD_DIM, HEAD_DIM), HEAD_DIM)
            scaled = dqr[h, j].astype(F32) * gain_s[pl.ds(j * heads + h, 1), :]
            acc = acc + scaled * x_s[:, columns].astype(F32)
        acc_s[...] = acc
        return carry

    lax.fori_loop(0, heads, arrived, 0)
    inv = inv_s[...]
    shift = jnp.sum(acc_s[...], axis=1, keepdims=True) * (1.0 / features) * (inv * inv * inv)
    acc_s[...] = shift

    def store_out(j):
        columns = pl.ds(pl.multiple_of(j * width, HEAD_DIM), width)
        return pltpu.make_async_copy(out_b.at[:, columns], gi_hbm.at[:, columns], out_sem.at[j])

    def finish(j, carry):
        inv = inv_s[...]
        shift = acc_s[...]
        for h in range(heads):
            columns = pl.ds(pl.multiple_of((j * heads + h) * HEAD_DIM, HEAD_DIM), HEAD_DIM)
            scaled = dqr[h, j].astype(F32) * gain_s[pl.ds(j * heads + h, 1), :]
            x = x_s[:, columns].astype(F32)
            out = up[h, j].astype(F32) + (scaled * inv - x * shift)
            out_b[:, columns] = out.astype(BF16)
        store_out(j).start()
        return carry

    lax.fori_loop(0, n_t, finish, 0)

    share.wait()
    summed = pg[...] + pgr[...]
    for h in range(heads):
        gg_ref[:, h * HEAD_DIM : (h + 1) * HEAD_DIM] = summed[h : h + 1, :]

    def drain(h, carry):
        many = pl.ds(0, n_t - 1)
        pltpu.make_async_copy(nb.at[h, many], nb.at[h, many], nb_send.at[h]).wait()
        pltpu.make_async_copy(up.at[h], up.at[h], up_send.at[h]).wait()
        pltpu.make_async_copy(nb.at[h, many], nb.at[h, many], go_send.at[h]).wait()
        pltpu.make_async_copy(nb.at[h, many], nb.at[h, many], dq_send.at[h]).wait()
        store_dk(h).wait()
        store_dv(h).wait()
        return carry

    lax.fori_loop(0, heads, drain, 0)

    def drain_out(j, carry):
        store_out(j).wait()
        return carry

    lax.fori_loop(0, n_t, drain_out, 0)


def body(n_pipe, n_t, upstream, inputs, keys, values, gain):
    tokens, features = inputs.shape[2:]
    length, width = keys.shape[2:]
    heads = width // HEAD_DIM
    dma = pltpu.SemaphoreType.DMA
    rounds = pltpu.VMEM((heads, n_t, tokens, HEAD_DIM), BF16)
    by_head = pltpu.VMEM((heads, length, HEAD_DIM), BF16)
    anywhere = pl.BlockSpec(memory_space=pl.ANY)
    grad_inputs, grad_keys, grad_values, grad_gain = pl.pallas_call(
        functools.partial(kernel, n_pipe, n_t, heads),
        out_shape=(
            jax.ShapeDtypeStruct((tokens, features), BF16),
            jax.ShapeDtypeStruct((length, width), BF16),
            jax.ShapeDtypeStruct((length, width), BF16),
            jax.ShapeDtypeStruct((1, width), F32),
        ),
        in_specs=[anywhere] * 5,
        out_specs=(anywhere, anywhere, anywhere, pl.BlockSpec(memory_space=pltpu.VMEM)),
        scratch_shapes=[
            pltpu.VMEM((tokens, features), BF16),
            pltpu.VMEM((n_t * heads, HEAD_DIM), F32),
            pltpu.VMEM((tokens, HEAD_DIM), F32),
            rounds, by_head, rounds, by_head, by_head, rounds,
            by_head, by_head,
            pltpu.VMEM((length, HEAD_DIM), BF16),
            pltpu.VMEM((HEAD_DIM, length), BF16),
            pltpu.VMEM((length, ROWS), F32),
            pltpu.VMEM((length, ROWS), F32),
            pltpu.VMEM((length, HEAD_DIM), F32),
            pltpu.VMEM((length, HEAD_DIM), F32),
            by_head, by_head,
            pltpu.VMEM((tokens, HEAD_DIM), F32),
            pltpu.VMEM((tokens, features), BF16),
            pltpu.VMEM((8, HEAD_DIM), F32),
            pltpu.VMEM((8, HEAD_DIM), F32),
            dma, dma,
            dma((heads,)), dma((heads,)),
            dma((heads,)), dma((heads,)), dma((heads,)), dma((heads,)),
            dma((heads,)), dma((heads,)), dma((heads,)), dma((heads,)),
            dma, dma,
            dma((heads,)), dma((heads,)), dma((n_t,)),
        ],
        compiler_params=pltpu.CompilerParams(
            collective_id=0, has_side_effects=True, vmem_limit_bytes=48 * 2**20
        ),
    )(
        upstream.reshape(tokens, features),
        inputs.reshape(tokens, features),
        keys.reshape(length, width),
        values.reshape(length, width),
        gain.reshape(n_t * heads, HEAD_DIM),
    )
    return (
        grad_inputs.reshape(inputs.shape),
        grad_keys.reshape(keys.shape),
        grad_values.reshape(values.shape),
        grad_gain,
    )


def solution(mesh):
    in_specs = (
        P("pipe", "dp", "tensor", None),
        P("pipe", "dp", "tensor", None),
        P("pipe", "dp", None, "tensor"),
        P("pipe", "dp", None, "tensor"),
        P("pipe", None),
    )
    out_specs = (
        P("pipe", "dp", "tensor", None),
        P("pipe", "dp", None, "tensor"),
        P("pipe", "dp", None, "tensor"),
        P("pipe", "tensor"),
    )
    step = functools.partial(body, mesh.shape["pipe"], mesh.shape["tensor"])
    return jax.shard_map(step, mesh=mesh, in_specs=in_specs, out_specs=out_specs, check_vma=False)
```

time: 647 us -> 75.2 us (0.12); the launches traced: 637 us -> 75.1 us
  waiting for transfers between devices: 251 us -> 0 us
  matrix products: 164 us -> 0 us
  local copies, waits for them, and re-layouts: 105 us -> 4.74 us
  other arithmetic: 76.6 us -> 0 us
  Pallas kernels: 0 us -> 69.7 us
  starting transfers between devices: 16 us -> 0 us
  between operations: 14.5 us -> 0.65 us
  blocking collectives: 8.27 us -> 0 us
    dot_general x10 -> x0, matrix products: 164 us -> none  [the longest x2 70.7 us: block_step(): jnp.einsum('mhqk,mqhd->mkhd', grad_scores, query_block, preferred_element...]
    ppermute x1 -> x0, waiting for transfers between devices: 157 us -> none  [from_behind(): lax.ppermute(x, axis, [(i, (i + by) % devices) for i in range(devices)])]
    all_gather x1 -> x0, waiting for transfers between devices: 79.4 us -> none  [body(): full_rows = lax.all_gather(upstream, 'tensor', axis=2, tiled=True)]
    pallas_call x0 -> x1, Pallas kernels: none -> 69.7 us  [body(): pl.pallas_call(functools.partial(kernel, n_pipe, n_t, heads), out_shape=(...]
    unnamed x4 -> x0, other arithmetic: 45.8 us -> none
    convert_element_type x5 -> x0, local copies, waits for them, and re-layouts: 37.7 us -> none  [the longest x1 25.2 us: body(): normed_b = normed.astype(jnp.bfloat16)]
    unnamed x36 -> x6, local copies, waits for them, and re-layouts: 41 us -> 4.74 us
    convert_element_type x7 -> x0, other arithmetic: 15.5 us -> none  [the longest x1 4.08 us: body(): (normed_heads.astype(jnp.float32) * gain_columns[:, None, None, :]).astyp...]
  transfers between devices with their start and end apart: 4 -> 0, of which waited for: 3 -> 0; matrix products, arithmetic and copies ran while one was open for 19% -> 0% of each run, Pallas kernels for 0% -> 0%
where the time goes in v1:
time: 75.2 us; the launch traced here: 75.1 us
  Pallas kernels  69.7 us (93%)
  local copies, waits for them, and re-layouts  4.74 us (6%)
    pallas_call x1, Pallas kernels, body(): pl.pallas_call(functools.partial(kernel, n_pipe, n_t, heads), out_shape=(...  69.7 us
    unnamed x6, local copies, waits for them, and re-layouts  4.74 us

profile of v1, /device:TPU:1, one launch (start us, length us, event | category | flops | bytes accessed | tf_op | source)
XLA Modules:
  0.0 75.1 jit_solution(8964113629232667600)
XLA Ops:
  0.6 0.0 copy-start
  0.6 0.7 copy-done
  1.4 69.7 %shard_map.84 = (bf16[128,6144]{1,0:T(8,128)(2,1)S(1)}, bf16[1024,768]{1,0:T(8,128)(2,1)S(1)}, bf16[1024,768]{1,0:T(8,128)(2,1)S(1)}, f32[1,768]{1,0:T(1,128)S(1)}) custom-call(bf16[128,6144]{1,0:T(8,128)(2,1)} %bitcast.12, bf16[128,6144]{1,0:T(8,128)(2,1)} %bitcast.13, bf16[1024,768]{1,0:T(8,128)(2,1)} %bitcast.14, bf16[1024,768]{1,0:T(8,128)(2,1)} %bitcast.15, ...), custom_call_target="tpu_custom_call" | custom-call | tf_op jit(solution)/shard_map/pallas_call | solution.py:318
  71.0 1.1 %copy.13 = bf16[1,1,128,6144]{3,2,1,0:T(8,128)(2,1)} copy(bf16[1,1,128,6144]{3,2,1,0:T(8,128)(2,1)S(1)} %bitcast.10) | data formatting | bytes 3145728
  72.2 1.1 %copy.14 = bf16[1,1,1024,768]{3,2,1,0:T(8,128)(2,1)} copy(bf16[1,1,1024,768]{3,2,1,0:T(8,128)(2,1)S(1)} %bitcast.9) | data formatting | bytes 3145728
  73.3 1.1 %copy.15 = bf16[1,1,1024,768]{3,2,1,0:T(8,128)(2,1)} copy(bf16[1,1,1024,768]{3,2,1,0:T(8,128)(2,1)S(1)} %bitcast.8) | data formatting | bytes 3145728
  74.5 0.6 copy.16
Async XLA Ops:
  0.6 0.7 copy-start

commit v2 on v1

--- a/solution.py
+++ b/solution.py
@@ -12,6 +12,9 @@
 HEAD_DIM = 128
 EPSILON = 1e-05
 ROWS = 256
+FIRST = 4
+AHEAD = 3
+PIECES = 4
 F32 = jnp.float32
 BF16 = jnp.bfloat16
 
@@ -30,11 +33,11 @@
 def kernel(
     n_pipe, n_t, heads,
     up_hbm, x_hbm, k_hbm, v_hbm, gain_hbm,
-    gi_hbm, dk_hbm, dv_hbm, gg_ref,
-    x_s, gain_s, inv_s, nb, qn, up, go, dqs, dqr, k_s, v_s, q_s, kt_s,
-    s_s, d_s, dk_acc, dv_acc, dk_b, dv_b, acc_s, out_b, pg, pgr,
+    part_ref, x_s, shift_ref, dk_ref, dv_ref, gg_ref,
+    gain_s, inv_s, nb, qn, up, go, dqs, dqr, k_s, v_s, q_s, kt_s,
+    s_s, d_s, dk_acc, dv_acc, acc_s, pg, pgr,
     x_sem, gain_sem, k_sem, v_sem, nb_send, qn_recv, up_send, up_recv,
-    go_send, go_recv, dq_send, dq_recv, pg_send, pg_recv, dk_sem, dv_sem, out_sem,
+    go_send, go_recv, dq_send, dq_recv, pg_send, pg_recv, pair_sem,
 ):
     d = lax.axis_index("dp")
     p = lax.axis_index("pipe")
@@ -57,8 +60,10 @@
         return carry
 
     lax.fori_loop(1, n_t, greet, 0)
-    pl.semaphore_signal(barrier, inc=1, device_id=(d, after, t), device_id_type=MESH)
-    pl.semaphore_signal(barrier, inc=1, device_id=(1 - d, p, t), device_id_type=MESH)
+    second = lax.rem(t, 2)
+    own_second = t - second + 1
+    pl.semaphore_signal(barrier, inc=1, device_id=(d, after, own_second), device_id_type=MESH)
+    pl.semaphore_signal(barrier, inc=1, device_id=(1 - d, p, own_second), device_id_type=MESH)
 
     load_x = pltpu.make_async_copy(x_hbm, x_s, x_sem)
     load_x.start()
@@ -99,9 +104,7 @@
     lax.fori_loop(0, tokens // 16, norm_rows, 0)
     pg[...] = jnp.zeros_like(pg)
 
-    pl.semaphore_wait(barrier, n_t + 1)
-
-    def send_round(h, carry):
+    def send_normed_round(h):
         def send_normed(k, carry):
             to = peer(k)
             pltpu.make_async_remote_copy(
@@ -114,6 +117,7 @@
         lax.fori_loop(1, n_t, send_normed, 0)
         pltpu.make_async_copy(nb.at[h, t], qn.at[h, mine, :], qn_recv.at[h]).start()
 
+    def send_rows_round(h, carry):
         def send_rows(j, carry):
             columns = pl.ds(pl.multiple_of((j * heads + h) * HEAD_DIM, HEAD_DIM), HEAD_DIM)
             pltpu.make_async_remote_copy(
@@ -126,7 +130,23 @@
         lax.fori_loop(0, n_t, send_rows, 0)
         return carry
 
-    lax.fori_loop(0, heads, send_round, 0)
+    @pl.when(second == 0)
+    def _():
+        pl.semaphore_wait(barrier, n_t - 1)
+        for h in range(min(FIRST, heads)):
+            send_normed_round(h)
+        pl.semaphore_wait(pair_sem, 1)
+        lax.fori_loop(0, heads, send_rows_round, 0)
+
+    @pl.when(second == 1)
+    def _():
+        pl.semaphore_wait(barrier, n_t + 3)
+        pl.semaphore_signal(pair_sem, inc=1, device_id=(d, p, t - 1), device_id_type=MESH)
+        send_rows_round(0, 0)
+        for h in range(min(FIRST, heads)):
+            send_normed_round(h)
+        lax.fori_loop(1, heads, send_rows_round, 0)
+
     load_gain.wait()
 
     def relay(h):
@@ -143,6 +163,10 @@
 
         lax.fori_loop(1, n_t, send_grad, 0)
         pltpu.make_async_copy(up.at[h, t], go.at[h, mine, :], go_recv.at[h]).start()
+
+        @pl.when(h + FIRST < heads)
+        def _():
+            send_normed_round(h + FIRST)
 
     to_base2 = math.log2(math.e) / math.sqrt(HEAD_DIM)
     scaling = 1.0 / math.sqrt(HEAD_DIM)
@@ -197,33 +221,22 @@
         dqs[h, rows, :] = dq
         part = fold(dq.astype(F32) * qn[h, rows, :].astype(F32), jnp.sum)
         pg[pl.ds(h, 1), :] += jnp.sum(part, axis=0, keepdims=True)
-        for b in range(ROWS // tokens):
-            to = i * (ROWS // tokens) + b
-            block = dqs.at[h, pl.ds(to * tokens, tokens), :]
-
-            @pl.when(to != t)
-            def _():
-                pltpu.make_async_remote_copy(
-                    src_ref=block, dst_ref=dqr.at[h, t],
-                    send_sem=dq_send.at[h], recv_sem=dq_recv.at[h],
-                    device_id=(d, p, to), device_id_type=MESH,
-                ).start()
-
-            @pl.when(to == t)
-            def _():
-                pltpu.make_async_copy(block, dqr.at[h, t], dq_recv.at[h]).start()
-
-    def store_dk(h):
-        return pltpu.make_async_copy(dk_b.at[h], dk_hbm.at[:, head_columns(h)], dk_sem.at[h])
-
-    def store_dv(h):
-        return pltpu.make_async_copy(dv_b.at[h], dv_hbm.at[:, head_columns(h)], dv_sem.at[h])
+
+    def send_dq_round(h):
+        def send_dq(k, carry):
+            to = peer(k)
+            pltpu.make_async_remote_copy(
+                src_ref=dqs.at[h, pl.ds(pl.multiple_of(to * tokens, tokens), tokens), :],
+                dst_ref=dqr.at[h, t],
+                send_sem=dq_send.at[h], recv_sem=dq_recv.at[h],
+                device_id=(d, p, to), device_id_type=MESH,
+            ).start()
+            return carry
+
+        lax.fori_loop(1, n_t, send_dq, 0)
+        pltpu.make_async_copy(dqs.at[h, mine, :], dqr.at[h, t], dq_recv.at[h]).start()
 
     def head(h, carry):
-        @pl.when(h + 1 < heads)
-        def _():
-            relay(h + 1)
-
         load_k(h).wait()
         load_v(h).wait()
         kt_s[...] = k_s[h].T
@@ -233,13 +246,19 @@
         pltpu.make_async_copy(go.at[h], go.at[h], go_recv.at[h]).wait()
         for i in range(blocks):
             row_block(h, i)
-        dk_b[h] = dk_acc[...].astype(BF16)
-        dv_b[h] = dv_acc[...].astype(BF16)
-        store_dk(h).start()
-        store_dv(h).start()
-        return carry
-
-    relay(0)
+
+        send_dq_round(h)
+
+        @pl.when(h + AHEAD < heads)
+        def _():
+            relay(h + AHEAD)
+
+        dk_ref[:, head_columns(h)] = dk_acc[...].astype(BF16)
+        dv_ref[:, head_columns(h)] = dv_acc[...].astype(BF16)
+        return carry
+
+    for h in range(min(AHEAD, heads)):
+        relay(h)
     lax.fori_loop(0, heads, head, 0)
 
     share = pltpu.make_async_remote_copy(
@@ -253,35 +272,18 @@
     def arrived(h, carry):
         pltpu.make_async_copy(dqr.at[h], dqr.at[h], dq_recv.at[h]).wait()
         acc = acc_s[...]
+        inv = inv_s[...]
         for j in range(n_t):
             columns = pl.ds(pl.multiple_of((j * heads + h) * HEAD_DIM, HEAD_DIM), HEAD_DIM)
             scaled = dqr[h, j].astype(F32) * gain_s[pl.ds(j * heads + h, 1), :]
             acc = acc + scaled * x_s[:, columns].astype(F32)
+            part_ref[:, columns] = up[h, j].astype(F32) + scaled * inv
         acc_s[...] = acc
         return carry
 
     lax.fori_loop(0, heads, arrived, 0)
     inv = inv_s[...]
-    shift = jnp.sum(acc_s[...], axis=1, keepdims=True) * (1.0 / features) * (inv * inv * inv)
-    acc_s[...] = shift
-
-    def store_out(j):
-        columns = pl.ds(pl.multiple_of(j * width, HEAD_DIM), width)
-        return pltpu.make_async_copy(out_b.at[:, columns], gi_hbm.at[:, columns], out_sem.at[j])
-
-    def finish(j, carry):
-        inv = inv_s[...]
-        shift = acc_s[...]
-        for h in range(heads):
-            columns = pl.ds(pl.multiple_of((j * heads + h) * HEAD_DIM, HEAD_DIM), HEAD_DIM)
-            scaled = dqr[h, j].astype(F32) * gain_s[pl.ds(j * heads + h, 1), :]
-            x = x_s[:, columns].astype(F32)
-            out = up[h, j].astype(F32) + (scaled * inv - x * shift)
-            out_b[:, columns] = out.astype(BF16)
-        store_out(j).start()
-        return carry
-
-    lax.fori_loop(0, n_t, finish, 0)
+    shift_ref[...] = jnp.sum(acc_s[...], axis=1, keepdims=True) * (1.0 / features) * (inv * inv * inv)
 
     share.wait()
     summed = pg[...] + pgr[...]
@@ -294,17 +296,34 @@
         pltpu.make_async_copy(up.at[h], up.at[h], up_send.at[h]).wait()
         pltpu.make_async_copy(nb.at[h, many], nb.at[h, many], go_send.at[h]).wait()
         pltpu.make_async_copy(nb.at[h, many], nb.at[h, many], dq_send.at[h]).wait()
-        store_dk(h).wait()
-        store_dv(h).wait()
         return carry
 
     lax.fori_loop(0, heads, drain, 0)
 
-    def drain_out(j, carry):
-        store_out(j).wait()
-        return carry
-
-    lax.fori_loop(0, n_t, drain_out, 0)
+
+def finish_kernel(
+    part_ref, x_ref, shift_ref, dk_ref, dv_ref, gg_ref,
+    gi_out, dk_out, dv_out, gg_out, gi_b, sem, gi_sem,
+):
+    stores = [
+        pltpu.make_async_copy(dk_ref, dk_out, sem.at[0]),
+        pltpu.make_async_copy(dv_ref, dv_out, sem.at[1]),
+        pltpu.make_async_copy(gg_ref, gg_out, sem.at[2]),
+    ]
+    for store in stores:
+        store.start()
+    width = gi_b.shape[1] // PIECES
+    for j in range(PIECES):
+        for c in range(j * width, (j + 1) * width, HEAD_DIM):
+            columns = slice(c, c + HEAD_DIM)
+            out = part_ref[:, columns] - x_ref[:, columns].astype(F32) * shift_ref[...]
+            gi_b[:, columns] = out.astype(BF16)
+        columns = slice(j * width, (j + 1) * width)
+        store = pltpu.make_async_copy(gi_b.at[:, columns], gi_out.at[:, columns], gi_sem.at[j])
+        store.start()
+        stores.append(store)
+    for store in stores:
+        store.wait()
 
 
 def body(n_pipe, n_t, upstream, inputs, keys, values, gain):
@@ -315,18 +334,20 @@
     rounds = pltpu.VMEM((heads, n_t, tokens, HEAD_DIM), BF16)
     by_head = pltpu.VMEM((heads, length, HEAD_DIM), BF16)
     anywhere = pl.BlockSpec(memory_space=pl.ANY)
-    grad_inputs, grad_keys, grad_values, grad_gain = pl.pallas_call(
+    in_vmem = pl.BlockSpec(memory_space=pltpu.VMEM)
+    results = pl.pallas_call(
         functools.partial(kernel, n_pipe, n_t, heads),
         out_shape=(
-            jax.ShapeDtypeStruct((tokens, features), BF16),
-            jax.ShapeDtypeStruct((length, width), BF16),
-            jax.ShapeDtypeStruct((length, width), BF16),
-            jax.ShapeDtypeStruct((1, width), F32),
+            pltpu.VMEM((tokens, features), F32),
+            pltpu.VMEM((tokens, features), BF16),
+            pltpu.VMEM((tokens, HEAD_DIM), F32),
+            pltpu.VMEM((length, width), BF16),
+            pltpu.VMEM((length, width), BF16),
+            pltpu.VMEM((1, width), F32),
         ),
         in_specs=[anywhere] * 5,
-        out_specs=(anywhere, anywhere, anywhere, pl.BlockSpec(memory_space=pltpu.VMEM)),
+        out_specs=(in_vmem,) * 6,
         scratch_shapes=[
-            pltpu.VMEM((tokens, features), BF16),
             pltpu.VMEM((n_t * heads, HEAD_DIM), F32),
             pltpu.VMEM((tokens, HEAD_DIM), F32),
             rounds, by_head, rounds, by_head, by_head, rounds,
@@ -337,9 +358,7 @@
             pltpu.VMEM((length, ROWS), F32),
             pltpu.VMEM((length, HEAD_DIM), F32),
             pltpu.VMEM((length, HEAD_DIM), F32),
-            by_head, by_head,
             pltpu.VMEM((tokens, HEAD_DIM), F32),
-            pltpu.VMEM((tokens, features), BF16),
             pltpu.VMEM((8, HEAD_DIM), F32),
             pltpu.VMEM((8, HEAD_DIM), F32),
             dma, dma,
@@ -347,7 +366,7 @@
             dma((heads,)), dma((heads,)), dma((heads,)), dma((heads,)),
             dma((heads,)), dma((heads,)), dma((heads,)), dma((heads,)),
             dma, dma,
-            dma((heads,)), dma((heads,)), dma((n_t,)),
+            pltpu.SemaphoreType.REGULAR,
         ],
         compiler_params=pltpu.CompilerParams(
             collective_id=0, has_side_effects=True, vmem_limit_bytes=48 * 2**20
@@ -359,6 +378,20 @@
         values.reshape(length, width),
         gain.reshape(n_t * heads, HEAD_DIM),
     )
+    results = [pltpu.with_memory_space_constraint(r, pltpu.VMEM) for r in results]
+    grad_inputs, grad_keys, grad_values, grad_gain = pl.pallas_call(
+        finish_kernel,
+        out_shape=(
+            jax.ShapeDtypeStruct((tokens, features), BF16),
+            jax.ShapeDtypeStruct((length, width), BF16),
+            jax.ShapeDtypeStruct((length, width), BF16),
+            jax.ShapeDtypeStruct((1, width), F32),
+        ),
+        in_specs=[in_vmem] * 6,
+        out_specs=(anywhere,) * 4,
+        scratch_shapes=[pltpu.VMEM((tokens, features), BF16), dma((3,)), dma((PIECES,))],
+        compiler_params=pltpu.CompilerParams(vmem_limit_bytes=8 * 2**20),
+    )(*results)
     return (
         grad_inputs.reshape(inputs.shape),
         grad_keys.reshape(keys.shape),

time: 75.2 us -> 66.1 us (0.88)
  local copies, waits for them, and re-layouts: 4.74 us -> 0 us
  Pallas kernels: 69.7 us -> 65.3 us
    pallas_call x1, Pallas kernels: 69.7 us -> 63.1 us  [body(): pl.pallas_call(functools.partial(kernel, n_pipe, n_t, heads), out_shape=(...]
    unnamed x6 -> x0, local copies, waits for them, and re-layouts: 4.74 us -> none
    pallas_call x0 -> x1, Pallas kernels: none -> 2.24 us  [body(): pl.pallas_call(finish_kernel, out_shape=(jax.ShapeDtypeStruct((tokens, fe...]
where the time goes in v2:
time: 66.1 us; the launch traced here: 66 us
  Pallas kernels  65.3 us (99%)
    pallas_call x1, Pallas kernels, body(): pl.pallas_call(functools.partial(kernel, n_pipe, n_t, heads), out_shape=(...  63.1 us
    pallas_call x1, Pallas kernels, body(): pl.pallas_call(finish_kernel, out_shape=(jax.ShapeDtypeStruct((tokens, fe...  2.24 us

profile of v2, /device:TPU:1, one launch (start us, length us, event | category | flops | bytes accessed | tf_op | source)
XLA Modules:
  0.0 66.0 jit_solution(2367809887868916300)
XLA Ops:
  0.6 63.1 %shard_map.84 = (f32[128,6144]{1,0:T(8,128)S(1)}, bf16[128,6144]{1,0:T(8,128)(2,1)S(1)}, f32[128,128]{1,0:T(8,128)S(1)}, bf16[1024,768]{1,0:T(8,128)(2,1)S(1)}, ...) custom-call(bf16[128,6144]{1,0:T(8,128)(2,1)} %bitcast.8, bf16[128,6144]{1,0:T(8,128)(2,1)} %bitcast.9, ...), custom_call_target="tpu_custom_call" | custom-call | tf_op jit(solution)/shard_map/pallas_call | solution.py:338
  63.7 2.2 %shard_map.85 = (bf16[128,6144]{1,0:T(8,128)(2,1)}, bf16[1024,768]{1,0:T(8,128)(2,1)}, bf16[1024,768]{1,0:T(8,128)(2,1)}, f32[1,768]{1,0:T(1,128)}) custom-call(f32[128,6144]{1,0:T(8,128)S(1)} %get-tuple-element.14.part_ref, bf16[128,6144]{1,0:T(8,128)(2,1)S(1)} %get-tuple-element.15.x_ref, f32[128,128]{1,0:T(8,128)S(1)} %get-tuple-element.16.shift_ref, ...), custom_call_target="tpu_custom_call" | custom-call | tf_op jit(solution)/shard_map/pallas_call | solution.py:382

commit v3 on v2

--- a/solution.py
+++ b/solution.py
@@ -12,7 +12,7 @@
 HEAD_DIM = 128
 EPSILON = 1e-05
 ROWS = 256
-FIRST = 4
+FIRST = 5
 AHEAD = 3
 PIECES = 4
 F32 = jnp.float32
@@ -34,10 +34,10 @@
     n_pipe, n_t, heads,
     up_hbm, x_hbm, k_hbm, v_hbm, gain_hbm,
     part_ref, x_s, shift_ref, dk_ref, dv_ref, gg_ref,
-    gain_s, inv_s, nb, qn, up, go, dqs, dqr, k_s, v_s, q_s, kt_s,
+    gain_s, inv_s, inv_row, inv_rows, inv_all, xh, up, go, dqs, dqr, k_s, v_s, qn_s, q_s, kt_s,
     s_s, d_s, dk_acc, dv_acc, acc_s, pg, pgr,
-    x_sem, gain_sem, k_sem, v_sem, nb_send, qn_recv, up_send, up_recv,
-    go_send, go_recv, dq_send, dq_recv, pg_send, pg_recv, pair_sem,
+    x_sem, gain_sem, k_sem, v_sem, xh_send, xh_recv, up_send, up_recv,
+    go_send, go_recv, dq_send, dq_recv, pg_send, pg_recv, inv_send, inv_recv, pair_sem,
 ):
     d = lax.axis_index("dp")
     p = lax.axis_index("pipe")
@@ -51,7 +51,10 @@
     mine = pl.ds(pl.multiple_of(t * tokens, tokens), tokens)
 
     def peer(k):
-        return lax.rem(t + k, n_t)
+        return lax.rem(t + n_t - k, n_t)
+
+    def columns_of(j, h):
+        return pl.ds(pl.multiple_of((j * heads + h) * HEAD_DIM, HEAD_DIM), HEAD_DIM)
 
     barrier = pltpu.get_barrier_semaphore()
 
@@ -84,8 +87,50 @@
         load_v(h).start()
         return carry
 
+    load_x.wait()
     lax.fori_loop(0, heads, start_loads, 0)
-    load_x.wait()
+
+    def send_input_round(h):
+        def send_input(k, carry):
+            to = peer(k)
+            pltpu.make_async_remote_copy(
+                src_ref=x_s.at[:, columns_of(to, h)], dst_ref=xh.at[h, mine, :],
+                send_sem=xh_send.at[h], recv_sem=xh_recv.at[h],
+                device_id=(d, p, to), device_id_type=MESH,
+            ).start()
+            return carry
+
+        lax.fori_loop(1, n_t, send_input, 0)
+        pltpu.make_async_copy(x_s.at[:, columns_of(t, h)], xh.at[h, mine, :], xh_recv.at[h]).start()
+
+    def send_rows_round(h, carry):
+        def send_rows(j, carry):
+            pltpu.make_async_remote_copy(
+                src_ref=up_hbm.at[:, columns_of(j, h)], dst_ref=up.at[h, j],
+                send_sem=up_send.at[h], recv_sem=up_recv.at[h],
+                device_id=(d, before, t), device_id_type=MESH,
+            ).start()
+            return carry
+
+        lax.fori_loop(0, n_t, send_rows, 0)
+        return carry
+
+    @pl.when(second == 0)
+    def _():
+        pl.semaphore_wait(barrier, n_t - 1)
+        for h in range(min(FIRST, heads)):
+            send_input_round(h)
+        pl.semaphore_wait(pair_sem, 1)
+        lax.fori_loop(0, heads, send_rows_round, 0)
+
+    @pl.when(second == 1)
+    def _():
+        pl.semaphore_wait(barrier, n_t + 3)
+        pl.semaphore_signal(pair_sem, inc=1, device_id=(d, p, t - 1), device_id_type=MESH)
+        send_rows_round(0, 0)
+        for h in range(min(FIRST, heads)):
+            send_input_round(h)
+        lax.fori_loop(1, heads, send_rows_round, 0)
 
     def norm_rows(r, carry):
         rows = pl.ds(pl.multiple_of(r * 16, 16), 16)
@@ -94,59 +139,23 @@
             x = x_s[rows, c * HEAD_DIM : (c + 1) * HEAD_DIM].astype(F32)
             total = total + x * x
         mean = jnp.sum(total, axis=1, keepdims=True) * (1.0 / features)
-        inv = jnp.broadcast_to(1.0 / jnp.sqrt(mean + EPSILON), (16, HEAD_DIM))
-        inv_s[rows, :] = inv
-        for c in range(n_t * heads):
-            x = x_s[rows, c * HEAD_DIM : (c + 1) * HEAD_DIM].astype(F32)
-            nb[c % heads, c // heads, rows, :] = (x * inv).astype(BF16)
+        inv_s[rows, :] = jnp.broadcast_to(1.0 / jnp.sqrt(mean + EPSILON), (16, HEAD_DIM))
         return carry
 
     lax.fori_loop(0, tokens // 16, norm_rows, 0)
+    inv_row[...] = inv_s[...].T[:8, :]
+
+    def send_inv(k, carry):
+        to = peer(k)
+        pltpu.make_async_remote_copy(
+            src_ref=inv_row, dst_ref=inv_rows.at[t], send_sem=inv_send, recv_sem=inv_recv,
+            device_id=(d, p, to), device_id_type=MESH,
+        ).start()
+        return carry
+
+    lax.fori_loop(1, n_t, send_inv, 0)
+    pltpu.make_async_copy(inv_row, inv_rows.at[t], inv_recv).start()
     pg[...] = jnp.zeros_like(pg)
-
-    def send_normed_round(h):
-        def send_normed(k, carry):
-            to = peer(k)
-            pltpu.make_async_remote_copy(
-                src_ref=nb.at[h, to], dst_ref=qn.at[h, mine, :],
-                send_sem=nb_send.at[h], recv_sem=qn_recv.at[h],
-                device_id=(d, p, to), device_id_type=MESH,
-            ).start()
-            return carry
-
-        lax.fori_loop(1, n_t, send_normed, 0)
-        pltpu.make_async_copy(nb.at[h, t], qn.at[h, mine, :], qn_recv.at[h]).start()
-
-    def send_rows_round(h, carry):
-        def send_rows(j, carry):
-            columns = pl.ds(pl.multiple_of((j * heads + h) * HEAD_DIM, HEAD_DIM), HEAD_DIM)
-            pltpu.make_async_remote_copy(
-                src_ref=up_hbm.at[:, columns], dst_ref=up.at[h, j],
-                send_sem=up_send.at[h], recv_sem=up_recv.at[h],
-                device_id=(d, before, t), device_id_type=MESH,
-            ).start()
-            return carry
-
-        lax.fori_loop(0, n_t, send_rows, 0)
-        return carry
-
-    @pl.when(second == 0)
-    def _():
-        pl.semaphore_wait(barrier, n_t - 1)
-        for h in range(min(FIRST, heads)):
-            send_normed_round(h)
-        pl.semaphore_wait(pair_sem, 1)
-        lax.fori_loop(0, heads, send_rows_round, 0)
-
-    @pl.when(second == 1)
-    def _():
-        pl.semaphore_wait(barrier, n_t + 3)
-        pl.semaphore_signal(pair_sem, inc=1, device_id=(d, p, t - 1), device_id_type=MESH)
-        send_rows_round(0, 0)
-        for h in range(min(FIRST, heads)):
-            send_normed_round(h)
-        lax.fori_loop(1, heads, send_rows_round, 0)
-
     load_gain.wait()
 
     def relay(h):
@@ -166,7 +175,7 @@
 
         @pl.when(h + FIRST < heads)
         def _():
-            send_normed_round(h + FIRST)
+            send_input_round(h + FIRST)
 
     to_base2 = math.log2(math.e) / math.sqrt(HEAD_DIM)
     scaling = 1.0 / math.sqrt(HEAD_DIM)
@@ -219,7 +228,7 @@
             dq_t = dq_t + dot(kt_s[:, keys], grad_s, NN)
         dq = dq_t.T.astype(BF16)
         dqs[h, rows, :] = dq
-        part = fold(dq.astype(F32) * qn[h, rows, :].astype(F32), jnp.sum)
+        part = fold(dq.astype(F32) * qn_s[rows, :].astype(F32), jnp.sum)
         pg[pl.ds(h, 1), :] += jnp.sum(part, axis=0, keepdims=True)
 
     def send_dq_round(h):
@@ -240,9 +249,11 @@
         load_k(h).wait()
         load_v(h).wait()
         kt_s[...] = k_s[h].T
-        pltpu.make_async_copy(qn.at[h], qn.at[h], qn_recv.at[h]).wait()
+        pltpu.make_async_copy(xh.at[h], xh.at[h], xh_recv.at[h]).wait()
         gain_row = gain_s[pl.ds(t * heads + h, 1), :]
-        q_s[...] = (qn[h].astype(F32) * gain_row).astype(BF16)
+        normed = (xh[h].astype(F32) * inv_all[...]).astype(BF16)
+        qn_s[...] = normed
+        q_s[...] = (normed.astype(F32) * gain_row).astype(BF16)
         pltpu.make_async_copy(go.at[h], go.at[h], go_recv.at[h]).wait()
         for i in range(blocks):
             row_block(h, i)
@@ -259,6 +270,11 @@
 
     for h in range(min(AHEAD, heads)):
         relay(h)
+
+    pltpu.make_async_copy(inv_rows, inv_rows, inv_recv).wait()
+    for j in range(n_t):
+        row = jnp.broadcast_to(inv_rows[j, :1, :], (HEAD_DIM, tokens))
+        inv_all[j * tokens : (j + 1) * tokens, :] = row.T
     lax.fori_loop(0, heads, head, 0)
 
     share = pltpu.make_async_remote_copy(
@@ -274,7 +290,7 @@
         acc = acc_s[...]
         inv = inv_s[...]
         for j in range(n_t):
-            columns = pl.ds(pl.multiple_of((j * heads + h) * HEAD_DIM, HEAD_DIM), HEAD_DIM)
+            columns = columns_of(j, h)
             scaled = dqr[h, j].astype(F32) * gain_s[pl.ds(j * heads + h, 1), :]
             acc = acc + scaled * x_s[:, columns].astype(F32)
             part_ref[:, columns] = up[h, j].astype(F32) + scaled * inv
@@ -291,14 +307,16 @@
         gg_ref[:, h * HEAD_DIM : (h + 1) * HEAD_DIM] = summed[h : h + 1, :]
 
     def drain(h, carry):
-        many = pl.ds(0, n_t - 1)
-        pltpu.make_async_copy(nb.at[h, many], nb.at[h, many], nb_send.at[h]).wait()
+        many = up.at[h, pl.ds(0, n_t - 1)]
+        pltpu.make_async_copy(many, many, xh_send.at[h]).wait()
         pltpu.make_async_copy(up.at[h], up.at[h], up_send.at[h]).wait()
-        pltpu.make_async_copy(nb.at[h, many], nb.at[h, many], go_send.at[h]).wait()
-        pltpu.make_async_copy(nb.at[h, many], nb.at[h, many], dq_send.at[h]).wait()
+        pltpu.make_async_copy(many, many, go_send.at[h]).wait()
+        pltpu.make_async_copy(many, many, dq_send.at[h]).wait()
         return carry
 
     lax.fori_loop(0, heads, drain, 0)
+    all_inv = inv_rows.at[pl.ds(0, n_t - 1)]
+    pltpu.make_async_copy(all_inv, all_inv, inv_send).wait()
 
 
 def finish_kernel(
@@ -350,8 +368,12 @@
         scratch_shapes=[
             pltpu.VMEM((n_t * heads, HEAD_DIM), F32),
             pltpu.VMEM((tokens, HEAD_DIM), F32),
-            rounds, by_head, rounds, by_head, by_head, rounds,
+            pltpu.VMEM((8, tokens), F32),
+            pltpu.VMEM((n_t, 8, tokens), F32),
+            pltpu.VMEM((length, HEAD_DIM), F32),
+            by_head, rounds, by_head, by_head, rounds,
             by_head, by_head,
+            pltpu.VMEM((length, HEAD_DIM), BF16),
             pltpu.VMEM((length, HEAD_DIM), BF16),
             pltpu.VMEM((HEAD_DIM, length), BF16),
             pltpu.VMEM((length, ROWS), F32),
@@ -365,7 +387,7 @@
             dma((heads,)), dma((heads,)),
             dma((heads,)), dma((heads,)), dma((heads,)), dma((heads,)),
             dma((heads,)), dma((heads,)), dma((heads,)), dma((heads,)),
-            dma, dma,
+            dma, dma, dma, dma,
             pltpu.SemaphoreType.REGULAR,
         ],
         compiler_params=pltpu.CompilerParams(

time: 66.1 us -> 64.6 us (0.977)
  Pallas kernels: 65.3 us -> 63.2 us
    pallas_call x1, Pallas kernels: 63.1 us -> 61 us  [body(): pl.pallas_call(functools.partial(kernel, n_pipe, n_t, heads), out_shape=(...]
where the time goes in v3:
time: 64.6 us; the launch traced here: 63.9 us
  Pallas kernels  63.2 us (98%)
    pallas_call x1, Pallas kernels, body(): pl.pallas_call(functools.partial(kernel, n_pipe, n_t, heads), out_shape=(...  61 us
    pallas_call x1, Pallas kernels, body(): pl.pallas_call(finish_kernel, out_shape=(jax.ShapeDtypeStruct((tokens, fe...  2.24 us

profile of v3, /device:TPU:1, one launch (start us, length us, event | category | flops | bytes accessed | tf_op | source)
XLA Modules:
  0.0 63.9 jit_solution(15589350846902785245)
XLA Ops:
  0.6 61.0 %shard_map.84 = (f32[128,6144]{1,0:T(8,128)S(1)}, bf16[128,6144]{1,0:T(8,128)(2,1)S(1)}, f32[128,128]{1,0:T(8,128)S(1)}, bf16[1024,768]{1,0:T(8,128)(2,1)S(1)}, ...) custom-call(bf16[128,6144]{1,0:T(8,128)(2,1)} %bitcast.8, bf16[128,6144]{1,0:T(8,128)(2,1)} %bitcast.9, ...), custom_call_target="tpu_custom_call" | custom-call | tf_op jit(solution)/shard_map/pallas_call | solution.py:356
  61.6 2.2 %shard_map.85 = (bf16[128,6144]{1,0:T(8,128)(2,1)}, bf16[1024,768]{1,0:T(8,128)(2,1)}, bf16[1024,768]{1,0:T(8,128)(2,1)}, f32[1,768]{1,0:T(1,128)}) custom-call(f32[128,6144]{1,0:T(8,128)S(1)} %get-tuple-element.14.part_ref, bf16[128,6144]{1,0:T(8,128)(2,1)S(1)} %get-tuple-element.15.x_ref, f32[128,128]{1,0:T(8,128)S(1)} %get-tuple-element.16.shift_ref, ...), custom_call_target="tpu_custom_call" | custom-call | tf_op jit(solution)/shard_map/pallas_call | solution.py:404

commit v4 on v3

--- a/solution.py
+++ b/solution.py
@@ -184,39 +184,48 @@
         jnp.int32, (ROWS, ROWS), 1
     )
 
-    def row_block(h, i):
-        rows = pl.ds(i * ROWS, ROWS)
-        q_i = q_s[rows, :]
-        g_i = go[h, rows, :]
+    def scores_of(h, i):
+        s_i = s_s.at[i % 2]
+        q_i = q_s[pl.ds(i * ROWS, ROWS), :]
         top = None
         for c in range(i + 1):
             keys = pl.ds(c * ROWS, ROWS)
             s = dot(k_s[h, keys, :], q_i, NT)
             if c == i:
                 s = jnp.where(below, s, -jnp.inf)
-            s_s[keys, :] = s
+            s_i[keys, :] = s
             m = fold(s, jnp.max)
             top = m if top is None else jnp.maximum(top, m)
-        top = jnp.max(top, axis=0, keepdims=True)
+        return jnp.max(top, axis=0, keepdims=True)
+
+    def weights_of(h, i, top):
+        s_i, d_i = s_s.at[i % 2], d_s.at[i % 2]
+        g_i = go[h, pl.ds(i * ROWS, ROWS), :]
         total = jnp.zeros((8, ROWS), F32)
         weighted = jnp.zeros((8, ROWS), F32)
         for c in range(i + 1):
             keys = pl.ds(c * ROWS, ROWS)
-            e = jnp.exp2((s_s[keys, :] - top) * to_base2)
+            e = jnp.exp2((s_i[keys, :] - top) * to_base2)
             dp = dot(v_s[h, keys, :], g_i, NT)
-            s_s[keys, :] = e
-            d_s[keys, :] = dp
+            s_i[keys, :] = e
+            d_i[keys, :] = dp
             total = total + fold(e, jnp.sum)
             weighted = weighted + fold(e * dp, jnp.sum)
         norm = 1.0 / jnp.sum(total, axis=0, keepdims=True)
-        delta = jnp.sum(weighted, axis=0, keepdims=True) * norm
+        return norm, jnp.sum(weighted, axis=0, keepdims=True) * norm
+
+    def grads_of(h, i, norm, delta):
+        rows = pl.ds(i * ROWS, ROWS)
+        s_i, d_i = s_s.at[i % 2], d_s.at[i % 2]
+        q_i = q_s[rows, :]
+        g_i = go[h, rows, :]
         norm_scaled = norm * scaling
         dq_t = jnp.zeros((HEAD_DIM, ROWS), F32)
         for c in range(i + 1):
             keys = pl.ds(c * ROWS, ROWS)
-            e = s_s[keys, :]
+            e = s_i[keys, :]
             weights = (e * norm).astype(BF16)
-            grad_s = ((e * norm_scaled) * (d_s[keys, :] - delta)).astype(BF16)
+            grad_s = ((e * norm_scaled) * (d_i[keys, :] - delta)).astype(BF16)
             dv = dot(weights, g_i, NN)
             dk = dot(grad_s, q_i, NN)
             if c == i:
@@ -255,8 +264,11 @@
         qn_s[...] = normed
         q_s[...] = (normed.astype(F32) * gain_row).astype(BF16)
         pltpu.make_async_copy(go.at[h], go.at[h], go_recv.at[h]).wait()
+        ready = weights_of(h, 0, scores_of(h, 0))
         for i in range(blocks):
-            row_block(h, i)
+            after_i = weights_of(h, i + 1, scores_of(h, i + 1)) if i + 1 < blocks else None
+            grads_of(h, i, *ready)
+            ready = after_i
 
         send_dq_round(h)
 
@@ -376,8 +388,8 @@
             pltpu.VMEM((length, HEAD_DIM), BF16),
             pltpu.VMEM((length, HEAD_DIM), BF16),
             pltpu.VMEM((HEAD_DIM, length), BF16),
-            pltpu.VMEM((length, ROWS), F32),
-            pltpu.VMEM((length, ROWS), F32),
+            pltpu.VMEM((2, length, ROWS), F32),
+            pltpu.VMEM((2, length, ROWS), F32),
             pltpu.VMEM((length, HEAD_DIM), F32),
             pltpu.VMEM((length, HEAD_DIM), F32),
             pltpu.VMEM((tokens, HEAD_DIM), F32),

time: 64.6 us -> 64.3 us (level); the launches traced: 63.9 us -> 64.2 us
  no operation moved by 1% of the time
where the time goes in v4:
time: 64.3 us; the launch traced here: 64.2 us
  Pallas kernels  63.6 us (99%)
    pallas_call x1, Pallas kernels, body(): pl.pallas_call(functools.partial(kernel, n_pipe, n_t, heads), out_shape=(...  61.4 us
    pallas_call x1, Pallas kernels, body(): pl.pallas_call(finish_kernel, out_shape=(jax.ShapeDtypeStruct((tokens, fe...  2.24 us

profile of v4, /device:TPU:1, one launch (start us, length us, event | category | flops | bytes accessed | tf_op | source)
XLA Modules:
  0.0 64.2 jit_solution(75544159758334897)
XLA Ops:
  0.6 61.4 %shard_map.84 = (f32[128,6144]{1,0:T(8,128)S(1)}, bf16[128,6144]{1,0:T(8,128)(2,1)S(1)}, f32[128,128]{1,0:T(8,128)S(1)}, bf16[1024,768]{1,0:T(8,128)(2,1)S(1)}, ...) custom-call(bf16[128,6144]{1,0:T(8,128)(2,1)} %bitcast.8, bf16[128,6144]{1,0:T(8,128)(2,1)} %bitcast.9, ...), custom_call_target="tpu_custom_call" | custom-call | tf_op jit(solution)/shard_map/pallas_call | solution.py:368
  62.0 2.2 %shard_map.85 = (bf16[128,6144]{1,0:T(8,128)(2,1)}, bf16[1024,768]{1,0:T(8,128)(2,1)}, bf16[1024,768]{1,0:T(8,128)(2,1)}, f32[1,768]{1,0:T(1,128)}) custom-call(f32[128,6144]{1,0:T(8,128)S(1)} %get-tuple-element.14.part_ref, bf16[128,6144]{1,0:T(8,128)(2,1)S(1)} %get-tuple-element.15.x_ref, f32[128,128]{1,0:T(8,128)S(1)} %get-tuple-element.16.shift_ref, ...), custom_call_target="tpu_custom_call" | custom-call | tf_op jit(solution)/shard_map/pallas_call | solution.py:416
